TPU v7x, 256 devices: a whole 4x4x8 slice. The times are simulated.
256 devices in a mesh: vir: 32 (over x, z), occ: 4 (over y), rep: 2 (over core).
Axes of the slice: x: 4, y: 4, z: 8, core: 2. Of those that a mesh axis runs over, the one named last changes fastest.
Arguments:
- amplitudes: float32 [256, 64, 4096], P('vir', ('occ', 'rep')), may hold values from -6 to 6
- integrals: float32 [384, 512, 4096], P('vir', None, ('occ', 'rep')), may hold values from -0.005859375 to 0.005859375
- block_owner: int32 [256], replicated, may hold values from 0 to 31, as said below
Outputs:
- ladder: float32 [64, 512], P('occ', 'rep')
Inputs may be any that keep to these rules, and one draw needn't show every extreme that they name: `block_owner`: blocks 8 * s to 8 * s + 7 start on vir index s. No vir index owns more than 12 blocks and some owns exactly 12; slots beyond an index's count are unused. No vir index's starting blocks name one owner more than 2 times, and each names some owner exactly 2 times.
All inputs are finite; a program needn't handle non-finite values.
Results may differ from a plain program's by a relative error of at most 0.0001.
Values sent between devices are 32-bit elements; how exact they have to be, the bound alone decides.
No kernel may reach another device: no remote copies, remote signals or barrier semaphores. Data moves between devices by JAX's collectives and lax.ppermute only.
A program may use at most 128 MiB of HBM per device.

v0:
```python
import jax
import jax.numpy as jnp
from jax import lax
from jax.sharding import PartitionSpec as P


def block_ranks(owners, blocks_dev):
    block_ids = jnp.arange(owners.shape[0], dtype=jnp.int32)
    earlier = block_ids[None, :] < block_ids[:, None]
    same_owner = owners[None, :] == owners[:, None]
    same_source = block_ids[None, :] // blocks_dev == block_ids[:, None] // blocks_dev
    owner_rank = jnp.sum(jnp.where(same_owner & earlier, 1, 0), axis=1).astype(jnp.int32)
    src_rank = jnp.sum(jnp.where(same_owner & earlier & same_source, 1, 0), axis=1).astype(
        jnp.int32
    )
    return (owner_rank, src_rank)


def contract(owned, integrals):
    return jnp.einsum(
        "vpx,vax->pa",
        owned,
        integrals,
        precision=lax.Precision.HIGHEST,
        preferred_element_type=jnp.float32,
    )


def on_device(amplitudes, integrals, block_owner):
    vir_count = lax.axis_size("vir")
    blocks_dev = amplitudes.shape[0]
    slot_count = integrals.shape[0]
    capacity = max(2, 3 * blocks_dev // (2 * vir_count))
    vir_index = lax.axis_index("vir")
    owner_rank, src_rank = block_ranks(block_owner, blocks_dev)
    block_ids = jnp.arange(block_owner.shape[0], dtype=jnp.int32)
    is_mine = block_owner == vir_index
    slot_pick = is_mine[None, :] & (
        owner_rank[None, :] == jnp.arange(slot_count, dtype=jnp.int32)[:, None]
    )
    slot_live = jnp.sum(jnp.where(slot_pick, 1, 0), axis=1)
    chosen = jnp.sum(jnp.where(slot_pick, block_ids[None, :], 0), axis=1)
    flat_index = chosen // blocks_dev * capacity + src_rank[chosen]
    slot_mask = slot_live.astype(jnp.float32)[:, None, None]
    local_ids = vir_index * blocks_dev + jnp.arange(blocks_dev, dtype=jnp.int32)
    target = block_owner[local_ids]
    target_rank = src_rank[local_ids]
    target_hit = (
        target[None, None, :] == jnp.arange(vir_count, dtype=jnp.int32)[:, None, None]
    ) & (target_rank[None, None, :] == jnp.arange(capacity, dtype=jnp.int32)[None, :, None])
    send_index = jnp.sum(
        jnp.where(target_hit, jnp.arange(blocks_dev, dtype=jnp.int32)[None, None, :], 0), axis=2
    )
    send_live = jnp.sum(jnp.where(target_hit, 1, 0), axis=2).astype(jnp.float32)
    outgoing = jnp.take(amplitudes, send_index, axis=0) * send_live[:, :, None, None]
    arrived = lax.all_to_all(outgoing, "vir", split_axis=0, concat_axis=0, tiled=True)
    row_stack = arrived.reshape((arrived.shape[0] * arrived.shape[1],) + arrived.shape[2:])
    owned = jnp.take(row_stack, flat_index, axis=0) * slot_mask
    owned = lax.all_to_all(owned, ("occ", "rep"), split_axis=2, concat_axis=1, tiled=True)
    partial_value = contract(owned, integrals)
    rep_part = lax.psum_scatter(partial_value, "rep", scatter_dimension=1, tiled=True)
    pair_part = lax.psum_scatter(rep_part, "occ", scatter_dimension=0, tiled=True)
    return lax.psum(pair_part, "vir")


def solution(mesh):
    in_specs = (P("vir", ("occ", "rep"), None), P("vir", None, ("occ", "rep")), P())
    out_specs = P("occ", "rep")
    return jax.shard_map(
        on_device, mesh=mesh, in_specs=in_specs, out_specs=out_specs, check_vma=False
    )
```

profile of v0, /device:TPU:0, one launch (start us, length us, event | category | flops | bytes accessed | tf_op | source)
XLA Modules:
  0.0 531.7 jit_solution(18139110158587541731)
XLA Ops:
  6.5 0.0 copy-start
  6.6 1.0 select_reduce_fusion.1
  7.6 1.3 gather_fusion.1
  8.9 0.6 gather_fusion.2
  9.6 0.1 iota_compare_fusion.2
  9.7 0.1 fusion.8
  9.8 0.1 copy.20
  9.9 0.1 reshape.278
  10.0 0.1 copy.19
  10.1 0.1 copy.21
  10.2 0.0 copy-done
  10.2 4.3 gather_fusion.3
  14.5 8.5 %select_multiply_fusion = f32[32,2,8,4096]{3,2,1,0:T(8,128)} fusion(f32[32,2,8,4096]{3,2,1,0:T(8,128)} %bitcast.42, f32[32,2]{1,0:T(8,128)S(1)} %copy.21, pred[32,2]{1,0:T(8,128)(4,1)S(1)} %copy.19), kind=kLoop, calls=%fused_computation.5 | loop fusion | flops 4194304 | bytes 16777536 | tf_op jit(solution)/shard_map/mul | solution.py:55
  22.9 0.0 copy-start.2
  22.9 9.8 %all-to-all-start = ((f32[32,2,8,4096]{3,2,1,0:T(8,128)}), f32[32,2,8,4096]{3,2,1,0:T(8,128)}, u32[]{:S(2)}, u32[]{:S(2)}) async-start(f32[32,2,8,4096]{3,2,1,0:T(8,128)} %select_multiply_fusion), calls=%async_computation | async-start | bytes 16777216 | tf_op jit(solution)/shard_map/all_to_all | solution.py:56
  32.8 0.0 reduce-scatter.3.cloned.1.call-start
  32.8 0.0 copy-done.2
  32.9 0.1 select_reduce_fusion.2
  33.0 0.7 gather_fusion
  33.7 187.9 %all-to-all-done = f32[32,2,8,4096]{3,2,1,0:T(8,128)} async-done(((f32[32,2,8,4096]{3,2,1,0:T(8,128)}), f32[32,2,8,4096]{3,2,1,0:T(8,128)}, u32[]{:S(2)}, u32[]{:S(2)}) %all-to-all-start) | async-done | bytes 8388640 | tf_op jit(solution)/shard_map/all_to_all | solution.py:56
  221.6 5.3 gather_fusion.4
  226.9 1.6 select_multiply_fusion.1
  228.5 9.0 %copy.22 = f32[12,8,4096]{0,1,2:T(8,128)} copy(f32[12,8,4096]{2,1,0:T(8,128)S(1)} %select_multiply_fusion.1) | data formatting | bytes 3145728 | tf_op jit(solution)/shard_map/mul | solution.py:58
  237.5 18.2 %reshape.294 = f32[8,1,49152]{2,1,0:T(1,128)S(1)} reshape(f32[4096,8,12]{2,1,0:T(8,128)} %bitcast.40) | data formatting | bytes 3145728
  255.7 26.2 %all_to_all.23 = f32[8,1,49152]{2,1,0:T(1,128)} all-to-all(f32[8,1,49152]{2,1,0:T(1,128)S(1)} %reshape.294), channel_id=1, replica_groups=mesh['vir'=32,'occ'=4,'rep'=2] {'occ','rep'}, dimensions={0} | all-to-all | bytes 3145728 | tf_op jit(solution)/shard_map/all_to_all | solution.py:59
  281.9 0.5 broadcast.330
  282.4 5.8 %reduce = f32[8,49152]{1,0:T(8,128)S(1)} reduce(f32[8,1,49152]{2,1,0:T(1,128)} %all_to_all.23, f32[]{:T(128)} %broadcast.330), dimensions={1}, to_apply=%all_to_all.17.reduce_sub_computation | reduce | bytes 3145732 | tf_op jit(solution)/shard_map/all_to_all | solution.py:59
  288.2 24.4 %reshape.295 = f32[4096,8,12]{2,1,0:T(8,128)} reshape(f32[8,49152]{1,0:T(8,128)S(1)} %reduce) | data formatting | bytes 3145728
  312.6 0.0 copy-start.1
  312.6 10.2 %copy.23 = f32[12,8,8,512]{3,1,2,0:T(8,128)S(1)} copy(f32[12,8,8,512]{0,1,3,2:T(8,128)} %bitcast.41) | data formatting | bytes 3145728 | tf_op jit(solution)/shard_map/all_to_all | solution.py:59
  322.8 15.7 %fusion.2 = f32[64,512]{1,0:T(8,128)} fusion(f32[12,512,512]{2,1,0:T(8,128)} %param.4, f32[12,8,8,512]{3,1,2,0:T(8,128)S(1)} %copy.23), kind=kOutput, calls=%fused_computation.9 | convolution fusion | flops 2415919104 | bytes 14286848 | tf_op jit(solution)/shard_map/vpx,vax->pa/dot_general | solution.py:20
  338.5 0.0 reduce-scatter.3.cloned.1.call-update
  338.5 0.0 reduce-scatter.5.cloned.1.call-start
  338.6 16.5 %reduce-scatter.3.cloned.1.call-done = f32[64,256]{1,0:T(8,128)} async-done(((f32[64,512]{1,0:T(8,128)}), f32[64,256]{1,0:T(8,128)}) %reduce-scatter.3.cloned.1.call-update) | async-done | bytes 65552 | tf_op jit(solution)/shard_map/reduce_scatter | solution.py:61
  355.1 0.0 reduce-scatter.5.cloned.1.call-update
  355.1 26.6 %reduce-scatter.5.cloned.1.call-done = f32[16,256]{1,0:T(8,128)} async-done(((f32[64,256]{1,0:T(8,128)}), f32[16,256]{1,0:T(8,128)}) %reduce-scatter.5.cloned.1.call-update) | async-done | bytes 16400 | tf_op jit(solution)/shard_map/reduce_scatter | solution.py:62
  381.8 143.1 %psum.7 = f32[16,256]{1,0:T(8,128)} all-reduce(f32[16,256]{1,0:T(8,128)} %reduce-scatter.5.cloned.1.call-done), channel_id=1, replica_groups=mesh['vir'=32,'occ'=4,'rep'=2] {'vir'}, use_global_device_ids=true, to_apply=%region_8.9 | all-reduce | flops 4096 | bytes 32768 | tf_op jit(solution)/shard_map/psum | solution.py:63
  524.9 0.0 copy-done.1
  (15 shorter events, 0.1 us)
Async XLA Ops:
  6.5 3.6 copy-start
  22.9 9.9 %copy-start.2 = (s32[256]{0:T(256)S(1)}, s32[256]{0:T(256)}, u32[]{:S(2)}) copy-start(s32[256]{0:T(256)} %param.5) | copy-start | bytes 3076
  22.9 198.6 %all-to-all-start = ((f32[32,2,8,4096]{3,2,1,0:T(8,128)}), f32[32,2,8,4096]{3,2,1,0:T(8,128)}, u32[]{:S(2)}, u32[]{:S(2)}) async-start(f32[32,2,8,4096]{3,2,1,0:T(8,128)} %select_multiply_fusion), calls=%async_computation | async-start | bytes 16777216 | tf_op jit(solution)/shard_map/all_to_all | solution.py:56
  32.8 322.3 %reduce-scatter.3.cloned.1.call-start = ((), (), s32[]{:S(2)}) async-start(), calls=%async_computation.4 | async-start | bytes 196608 | tf_op jit(solution)/shard_map/reduce_scatter | solution.py:61
  312.6 212.3 %copy-start.1 = (f32[8,8,4096]{2,1,0:T(8,128)S(1)}, f32[8,8,4096]{2,1,0:T(8,128)}, u32[]{:S(2)}) copy-start(f32[8,8,4096]{2,1,0:T(8,128)} %param.3) | copy-start | bytes 3145732
  338.5 43.3 %reduce-scatter.5.cloned.1.call-start = ((), (), s32[]{:S(2)}) async-start(), calls=%async_computation.5 | async-start | bytes 81920 | tf_op jit(solution)/shard_map/reduce_scatter | solution.py:62
Sparse Core Ops, SparseCore 0:
  338.7 16.4 reduce-scatter.2
  357.6 24.1 reduce-scatter.4
where the time goes:
time: 532 us
  waiting for transfers between devices  231 us (43%)
  blocking collectives  169 us (32%)
  local copies, waits for them, and re-layouts  74.9 us (14%)
  other arithmetic  17.3 us (3%)
  matrix products  15.7 us (3%)
  between operations  13.5 us (3%)
  starting transfers between devices  9.92 us (2%)
    all_to_all x1, waiting for transfers between devices, on_device(): lax.all_to_all(outgoing, 'vir', split_axis=0, concat_axis=0, tiled=True)  188 us
    psum x1, blocking collectives, on_device(): return lax.psum(pair_part, 'vir')  143 us
    unnamed x8, local copies, waits for them, and re-layouts  42.6 us
    reduce_scatter x1, waiting for transfers between devices, on_device(): lax.psum_scatter(rep_part, 'occ', scatter_dimension=0, tiled=True)  26.6 us
    all_to_all x1, blocking collectives, on_device(): lax.all_to_all(owned, ('occ', 'rep'), split_axis=2, concat_axis=1, tiled=...  26.2 us
    reduce_scatter x1, waiting for transfers between devices, on_device(): lax.psum_scatter(partial_value, 'rep', scatter_dimension=1, tiled=True)  16.5 us
    dot_general x1, matrix products, contract(): jnp.einsum('vpx,vax->pa', owned, integrals, precision=lax.Precision.HIGHE...  15.7 us
    all_to_all x2, local copies, waits for them, and re-layouts, on_device(): lax.all_to_all(owned, ('occ', 'rep'), split_axis=2, concat_axis=1, tiled=...  10.7 us
  transfers between devices with their start and end apart: 3, of which 3 were waited for; matrix products, arithmetic and copies ran while one was open for 0% of the time, Pallas kernels for 0%

commit v1 on v0

--- a/solution.py
+++ b/solution.py
@@ -60,7 +60,7 @@
     partial_value = contract(owned, integrals)
     rep_part = lax.psum_scatter(partial_value, "rep", scatter_dimension=1, tiled=True)
     pair_part = lax.psum_scatter(rep_part, "occ", scatter_dimension=0, tiled=True)
-    return lax.psum(pair_part, "vir")
+    return jnp.sum(lax.all_gather(pair_part, "vir"), axis=0)
 
 
 def solution(mesh):

time: 532 us -> 441 us (0.83)
  blocking collectives: 169 us -> 76.4 us
    psum x1 -> x0, blocking collectives: 143 us -> none  [on_device(): return lax.psum(pair_part, 'vir')]
    all_gather x0 -> x1, blocking collectives: none -> 50.3 us  [on_device(): return jnp.sum(lax.all_gather(pair_part, 'vir'), axis=0)]
where the time goes in v1:
time: 441 us; the launch traced here: 440 us
  waiting for transfers between devices  231 us (52%)
  blocking collectives  76.4 us (17%)
  local copies, waits for them, and re-layouts  74.9 us (17%)
  other arithmetic  17.9 us (4%)
  matrix products  15.7 us (4%)
  between operations  13.5 us (3%)
  starting transfers between devices  9.92 us (2%)
    all_to_all x1, waiting for transfers between devices, on_device(): lax.all_to_all(outgoing, 'vir', split_axis=0, concat_axis=0, tiled=True)  188 us
    all_gather x1, blocking collectives, on_device(): return jnp.sum(lax.all_gather(pair_part, 'vir'), axis=0)  50.3 us
    unnamed x8, local copies, waits for them, and re-layouts  42.6 us
    reduce_scatter x1, waiting for transfers between devices, on_device(): lax.psum_scatter(rep_part, 'occ', scatter_dimension=0, tiled=True)  26.6 us
    all_to_all x1, blocking collectives, on_device(): lax.all_to_all(owned, ('occ', 'rep'), split_axis=2, concat_axis=1, tiled=...  26.2 us
    reduce_scatter x1, waiting for transfers between devices, on_device(): lax.psum_scatter(partial_value, 'rep', scatter_dimension=1, tiled=True)  16.5 us
    dot_general x1, matrix products, contract(): jnp.einsum('vpx,vax->pa', owned, integrals, precision=lax.Precision.HIGHE...  15.7 us
    all_to_all x2, local copies, waits for them, and re-layouts, on_device(): lax.all_to_all(owned, ('occ', 'rep'), split_axis=2, concat_axis=1, tiled=...  10.7 us
  transfers between devices with their start and end apart: 3, of which 3 were waited for; matrix products, arithmetic and copies ran while one was open for 0% of the time, Pallas kernels for 0%

profile of v1, /device:TPU:0, one launch (start us, length us, event | category | flops | bytes accessed | tf_op | source)
XLA Modules:
  0.0 439.5 jit_solution(9840816513684485242)
XLA Ops:
  6.5 0.0 copy-start
  6.6 1.0 select_reduce_fusion.1
  7.6 1.3 gather_fusion.1
  8.9 0.6 gather_fusion.2
  9.6 0.1 iota_compare_fusion.2
  9.7 0.1 fusion.8
  9.8 0.1 copy.20
  9.9 0.1 reshape.278
  10.0 0.1 copy.19
  10.1 0.1 copy.21
  10.2 0.0 copy-done
  10.2 4.3 gather_fusion.3
  14.5 8.5 %select_multiply_fusion = f32[32,2,8,4096]{3,2,1,0:T(8,128)} fusion(f32[32,2,8,4096]{3,2,1,0:T(8,128)} %bitcast.43, f32[32,2]{1,0:T(8,128)S(1)} %copy.21, pred[32,2]{1,0:T(8,128)(4,1)S(1)} %copy.19), kind=kLoop, calls=%fused_computation.5 | loop fusion | flops 4194304 | bytes 16777536 | tf_op jit(solution)/shard_map/mul | solution.py:55
  22.9 0.0 copy-start.2
  22.9 9.8 %all-to-all-start = ((f32[32,2,8,4096]{3,2,1,0:T(8,128)}), f32[32,2,8,4096]{3,2,1,0:T(8,128)}, u32[]{:S(2)}, u32[]{:S(2)}) async-start(f32[32,2,8,4096]{3,2,1,0:T(8,128)} %select_multiply_fusion), calls=%async_computation | async-start | bytes 16777216 | tf_op jit(solution)/shard_map/all_to_all | solution.py:56
  32.8 0.0 reduce-scatter.3.cloned.1.call-start
  32.8 0.0 copy-done.2
  32.9 0.1 select_reduce_fusion.2
  33.0 0.7 gather_fusion
  33.7 187.9 %all-to-all-done = f32[32,2,8,4096]{3,2,1,0:T(8,128)} async-done(((f32[32,2,8,4096]{3,2,1,0:T(8,128)}), f32[32,2,8,4096]{3,2,1,0:T(8,128)}, u32[]{:S(2)}, u32[]{:S(2)}) %all-to-all-start) | async-done | bytes 8388640 | tf_op jit(solution)/shard_map/all_to_all | solution.py:56
  221.6 5.3 %gather_fusion.4 = f32[12,8,4096]{2,1,0:T(8,128)} fusion(f32[64,8,4096]{2,1,0:T(8,128)} %bitcast.5, s32[1024]{0:T(1024)S(1)} %pad_clamp_fusion), kind=kCustom, calls=%fused_computation.4 | custom fusion | bytes 3145776 | tf_op jit(solution)/shard_map/jit(_take)/gather | solution.py:58
  226.9 1.6 select_multiply_fusion.1
  228.5 9.0 %copy.22 = f32[12,8,4096]{0,1,2:T(8,128)} copy(f32[12,8,4096]{2,1,0:T(8,128)S(1)} %select_multiply_fusion.1) | data formatting | bytes 3145728 | tf_op jit(solution)/shard_map/mul | solution.py:58
  237.5 18.2 %reshape.295 = f32[8,1,49152]{2,1,0:T(1,128)S(1)} reshape(f32[4096,8,12]{2,1,0:T(8,128)} %bitcast.41) | data formatting | bytes 3145728
  255.7 26.2 %all_to_all.23 = f32[8,1,49152]{2,1,0:T(1,128)} all-to-all(f32[8,1,49152]{2,1,0:T(1,128)S(1)} %reshape.295), channel_id=1, replica_groups=mesh['vir'=32,'occ'=4,'rep'=2] {'occ','rep'}, dimensions={0} | all-to-all | bytes 3145728 | tf_op jit(solution)/shard_map/all_to_all | solution.py:59
  281.9 0.5 broadcast.330
  282.4 5.8 %reduce = f32[8,49152]{1,0:T(8,128)S(1)} reduce(f32[8,1,49152]{2,1,0:T(1,128)} %all_to_all.23, f32[]{:T(128)} %broadcast.330), dimensions={1}, to_apply=%all_to_all.17.reduce_sub_computation | reduce | bytes 3145732 | tf_op jit(solution)/shard_map/all_to_all | solution.py:59
  288.2 24.4 %reshape.296 = f32[4096,8,12]{2,1,0:T(8,128)} reshape(f32[8,49152]{1,0:T(8,128)S(1)} %reduce) | data formatting | bytes 3145728
  312.6 0.0 copy-start.1
  312.6 10.2 %copy.23 = f32[12,8,8,512]{3,1,2,0:T(8,128)S(1)} copy(f32[12,8,8,512]{0,1,3,2:T(8,128)} %bitcast.42) | data formatting | bytes 3145728 | tf_op jit(solution)/shard_map/all_to_all | solution.py:59
  322.8 15.7 %fusion.2 = f32[64,512]{1,0:T(8,128)} fusion(f32[12,512,512]{2,1,0:T(8,128)} %param.4, f32[12,8,8,512]{3,1,2,0:T(8,128)S(1)} %copy.23), kind=kOutput, calls=%fused_computation.9 | convolution fusion | flops 2415919104 | bytes 14286848 | tf_op jit(solution)/shard_map/vpx,vax->pa/dot_general | solution.py:20
  338.5 0.0 reduce-scatter.3.cloned.1.call-update
  338.5 0.0 reduce-scatter.5.cloned.1.call-start
  338.6 16.5 %reduce-scatter.3.cloned.1.call-done = f32[64,256]{1,0:T(8,128)} async-done(((f32[64,512]{1,0:T(8,128)}), f32[64,256]{1,0:T(8,128)}) %reduce-scatter.3.cloned.1.call-update) | async-done | bytes 65552 | tf_op jit(solution)/shard_map/reduce_scatter | solution.py:61
  355.1 0.0 reduce-scatter.5.cloned.1.call-update
  355.1 26.6 %reduce-scatter.5.cloned.1.call-done = f32[16,256]{1,0:T(8,128)} async-done(((f32[64,256]{1,0:T(8,128)}), f32[16,256]{1,0:T(8,128)}) %reduce-scatter.5.cloned.1.call-update) | async-done | bytes 16400 | tf_op jit(solution)/shard_map/reduce_scatter | solution.py:62
  381.8 50.3 %all-gather = f32[512,256]{1,0:T(8,128)S(1)} all-gather(f32[16,256]{1,0:T(8,128)} %reduce-scatter.5.cloned.1.call-done), channel_id=2, replica_groups=mesh['vir'=32,'occ'=4,'rep'=2] {'vir'}, dimensions={0}, use_global_device_ids=true | all-gather | bytes 540672 | tf_op jit(solution)/shard_map/all_gather | solution.py:63
  432.1 0.7 reduce_sum.75
  432.7 0.0 copy-done.1
  (15 shorter events, 0.1 us)
Async XLA Ops:
  6.5 3.6 copy-start
  22.9 9.9 %copy-start.2 = (s32[256]{0:T(256)S(1)}, s32[256]{0:T(256)}, u32[]{:S(2)}) copy-start(s32[256]{0:T(256)} %param.5) | copy-start | bytes 3076
  22.9 198.6 %all-to-all-start = ((f32[32,2,8,4096]{3,2,1,0:T(8,128)}), f32[32,2,8,4096]{3,2,1,0:T(8,128)}, u32[]{:S(2)}, u32[]{:S(2)}) async-start(f32[32,2,8,4096]{3,2,1,0:T(8,128)} %select_multiply_fusion), calls=%async_computation | async-start | bytes 16777216 | tf_op jit(solution)/shard_map/all_to_all | solution.py:56
  32.8 322.3 %reduce-scatter.3.cloned.1.call-start = ((), (), s32[]{:S(2)}) async-start(), calls=%async_computation.4 | async-start | bytes 196608 | tf_op jit(solution)/shard_map/reduce_scatter | solution.py:61
  312.6 120.1 %copy-start.1 = (f32[8,8,4096]{2,1,0:T(8,128)S(1)}, f32[8,8,4096]{2,1,0:T(8,128)}, u32[]{:S(2)}) copy-start(f32[8,8,4096]{2,1,0:T(8,128)} %param.3) | copy-start | bytes 3145732
  338.5 43.3 %reduce-scatter.5.cloned.1.call-start = ((), (), s32[]{:S(2)}) async-start(), calls=%async_computation.5 | async-start | bytes 81920 | tf_op jit(solution)/shard_map/reduce_scatter | solution.py:62
Sparse Core Ops, SparseCore 0:
  338.7 16.4 reduce-scatter.2
  357.6 24.1 reduce-scatter.4
